TPU v7x, 32 devices: a whole 2x2x4 slice. The times are simulated.
32 devices in a mesh: dp: 4 (over z), section: 2 (over x), expert: 4 (over y, core).
Axes of the slice: x: 2, y: 2, z: 4, core: 2. Of those that a mesh axis runs over, the one named last changes fastest.
Arguments:
- act_in: bfloat16 [2, 1024, 2048], P('section', ('dp', 'expert')), may hold values from -6 to 6
- saved_in: bfloat16 [2, 1024, 2048], P('section', ('dp', 'expert')), may hold values from -6 to 6
- grad_in: bfloat16 [2, 1024, 2048], P('section', ('dp', 'expert')), may hold values from -6 to 6
- fwd_ids: int32 [2, 1024, 2], P('section', ('dp', 'expert')), may hold values from 0 to 3, all different within a row; in each aligned block of 64 rows (0 to 63, 64 to 127, ..., all dimensions but the last counted through in order) at most 40 rows name the same one
- bwd_ids: int32 [2, 1024, 2], P('section', ('dp', 'expert')), may hold values from 0 to 3, all different within a row; in each aligned block of 64 rows (0 to 63, 64 to 127, ..., all dimensions but the last counted through in order) at most 40 rows name the same one
- fwd_gates: float32 [2, 1024, 2], P('section', ('dp', 'expert')), may hold values from 0.2 to 1
- bwd_gates: float32 [2, 1024, 2], P('section', ('dp', 'expert')), may hold values from 0.2 to 1
- norm_gain: float32 [2, 2048], P('section'), may hold values from 0.5 to 1.5
- w_gate: bfloat16 [2, 4, 2048, 384], P('section', 'expert'), may hold values from -0.125 to 0.125
- w_up: bfloat16 [2, 4, 2048, 384], P('section', 'expert'), may hold values from -0.125 to 0.125
- w_down: bfloat16 [2, 4, 384, 2048], P('section', 'expert'), may hold values from -0.3125 to 0.3125
Outputs:
- act_out: bfloat16 [2, 1024, 2048], P('section', ('dp', 'expert'))
- grad_out: bfloat16 [2, 1024, 2048], P('section', ('dp', 'expert'))
- weight_grads: float32 [2, 4, 2048, 1152], P('section', 'expert', 'dp')
Inputs may be any that keep to these rules, and one draw needn't show every extreme that they name: `fwd_ids`: the 2 entries of a token name different experts. In each aligned block of 64 tokens of a section (the tokens of one device), no expert is named by more than 40 entries, and in every draw some block has an expert named exactly 40 times. `bwd_ids`: the 2 entries of a token name different experts. In each aligned block of 64 tokens of a section (the tokens of one device), no expert is named by more than 40 entries, and in every draw some block has an expert named exactly 40 times.
All inputs are finite; a program needn't handle non-finite values.
Results may differ from a plain program's by a relative error of at most 0.017.
Values may be sent and summed in bfloat16 or wider, within the bound.
A program may use at most 64 MiB of HBM per device.

v0:
```python
import jax
import jax.numpy as jnp
from jax import lax
from jax.sharding import PartitionSpec as P

EPS = 1e-06


def padded(block, sides, width):
    for axis, dim in sides:
        count = lax.axis_size(axis)
        forward = [(i, i + 1) for i in range(count - 1)]
        forward.append((count - 1, 0))
        backward = [(target, source) for source, target in forward]
        low = lax.ppermute(
            lax.slice_in_dim(block, block.shape[dim] - width, None, axis=dim), axis, forward
        )
        high = lax.ppermute(lax.slice_in_dim(block, 0, width, axis=dim), axis, backward)
        block = jnp.concatenate([low, block, high], axis=dim)
    return block


def rms_norm(rows, gain):
    wide = rows.astype(jnp.float32)
    factor = lax.rsqrt(jnp.mean(wide * wide, axis=-1, keepdims=True) + EPS)
    return wide * factor * gain


def place_rows(ids, experts, capacity):
    flat = ids.reshape(-1)
    onehot = (flat[:, None] == jnp.arange(experts, dtype=jnp.int32)[None, :]).astype(jnp.int32)
    before = jnp.cumsum(onehot, axis=0) - onehot
    slot = jnp.sum(before * onehot, axis=1)
    return flat * capacity + slot


def place_matrix(dest, experts, capacity):
    return (jnp.arange(experts * capacity, dtype=jnp.int32)[:, None] == dest[None, :]).astype(
        jnp.bfloat16
    )


def shards(
    act_in,
    saved_in,
    grad_in,
    fwd_ids,
    bwd_ids,
    fwd_gates,
    bwd_gates,
    norm_gain,
    w_gate,
    w_up,
    w_down,
):
    experts = lax.axis_size("expert")
    replicas = lax.axis_size("dp")
    tokens = act_in.shape[1]
    width = act_in.shape[2]
    topk = fwd_ids.shape[2]
    capacity = min(tokens, 5 * tokens * topk // (4 * experts))
    gain = norm_gain[0]
    weight_gate = w_gate[0, 0]
    weight_up = w_up[0, 0]
    weight_down = w_down[0, 0]
    here = act_in[0]
    upstream = grad_in[0].astype(jnp.float32)
    normed_fwd = rms_norm(here, gain).astype(jnp.bfloat16)
    normed_wide, pull_back = jax.vjp(lambda v: rms_norm(v, gain), saved_in[0].astype(jnp.float32))
    normed_bwd = normed_wide.astype(jnp.bfloat16)
    out_grad = (
        (bwd_gates[0][:, :, None] * upstream[:, None, :])
        .astype(jnp.bfloat16)
        .reshape(tokens * topk, width)
    )
    dest_fwd = place_rows(fwd_ids[0], experts, capacity)
    dest_bwd = place_rows(bwd_ids[0], experts, capacity)
    send_fwd = jnp.dot(
        place_matrix(dest_fwd, experts, capacity),
        jnp.repeat(normed_fwd, topk, axis=0),
        preferred_element_type=jnp.float32,
    ).astype(jnp.bfloat16)
    joined = jnp.concatenate([jnp.repeat(normed_bwd, topk, axis=0), out_grad], axis=1)
    send_joined = jnp.dot(
        place_matrix(dest_bwd, experts, capacity), joined, preferred_element_type=jnp.float32
    ).astype(jnp.bfloat16)
    send_bwd = send_joined[:, :width].reshape(experts, capacity, width)
    send_grad = send_joined[:, width:].reshape(experts, capacity, width)
    recv_fwd, recv_bwd, recv_grad = (
        lax.all_to_all(
            send_fwd.reshape(experts, capacity, width),
            "expert",
            split_axis=0,
            concat_axis=0,
            tiled=True,
        ),
        lax.all_to_all(send_bwd, "expert", split_axis=0, concat_axis=0, tiled=True),
        lax.all_to_all(send_grad, "expert", split_axis=0, concat_axis=0, tiled=True),
    )
    rows_fwd = recv_fwd.reshape(-1, width)
    rows_bwd = recv_bwd.reshape(-1, width)
    rows_grad = recv_grad.reshape(-1, width)
    pre_gate = jnp.dot(rows_fwd, weight_gate, preferred_element_type=jnp.float32)
    pre_up = jnp.dot(rows_fwd, weight_up, preferred_element_type=jnp.float32)
    hidden_fwd = (jax.nn.silu(pre_gate) * pre_up).astype(jnp.bfloat16)
    out_fwd = jnp.dot(hidden_fwd, weight_down, preferred_element_type=jnp.float32).astype(
        jnp.bfloat16
    )
    contract_last = (((1,), (1,)), ((), ()))
    back_gate = jnp.dot(rows_bwd, weight_gate, preferred_element_type=jnp.float32)
    back_up = jnp.dot(rows_bwd, weight_up, preferred_element_type=jnp.float32)
    sig = jax.nn.sigmoid(back_gate)
    silu_gate = jax.nn.silu(back_gate)
    hidden_bwd = (silu_gate * back_up).astype(jnp.bfloat16)
    hidden_grad = lax.dot_general(
        rows_grad, weight_down, contract_last, preferred_element_type=jnp.float32
    )
    gate_grad = (hidden_grad * back_up * sig * (1.0 + back_gate * (1.0 - sig))).astype(jnp.bfloat16)
    up_grad = (hidden_grad * silu_gate).astype(jnp.bfloat16)
    slot_grad = (
        lax.dot_general(gate_grad, weight_gate, contract_last, preferred_element_type=jnp.float32)
        + lax.dot_general(up_grad, weight_up, contract_last, preferred_element_type=jnp.float32)
    ).astype(jnp.bfloat16)
    back_fwd, back_grad = (
        lax.all_to_all(
            out_fwd.reshape(experts, capacity, width),
            "expert",
            split_axis=0,
            concat_axis=0,
            tiled=True,
        ),
        lax.all_to_all(
            slot_grad.reshape(experts, capacity, width),
            "expert",
            split_axis=0,
            concat_axis=0,
            tiled=True,
        ),
    )
    picked = back_fwd.reshape(-1, width)[dest_fwd].reshape(tokens, topk, width).astype(jnp.float32)
    layer_out = (
        here.astype(jnp.float32) + jnp.sum(fwd_gates[0][:, :, None] * picked, axis=1)
    ).astype(jnp.bfloat16)
    normed_grad = jnp.sum(
        back_grad.reshape(-1, width)[dest_bwd].reshape(tokens, topk, width).astype(jnp.float32),
        axis=1,
    )
    input_grad = (upstream + pull_back(normed_grad)[0]).astype(jnp.bfloat16)
    passed = padded(jnp.stack([input_grad, layer_out]), (("section", 0),), 1)
    act_out = passed[0][None]
    grad_out = passed[3][None]
    scale = 1.0 / replicas
    contract_first = (((0,), (0,)), ((), ()))
    slot_rows = rows_bwd.shape[0]
    hid = hidden_bwd.shape[1]
    upper_right = jnp.concatenate(
        [gate_grad, up_grad, jnp.zeros((slot_rows, hid), jnp.bfloat16)], axis=1
    )
    lower_right = jnp.concatenate(
        [jnp.zeros((slot_rows, 2 * hid), jnp.bfloat16), hidden_bwd], axis=1
    )
    right_blocks = jnp.concatenate([upper_right, lower_right], axis=0)
    left_rows = jnp.concatenate([rows_bwd, rows_grad], axis=0)
    summed = lax.psum_scatter(
        (
            lax.dot_general(
                left_rows, right_blocks, contract_first, preferred_element_type=jnp.float32
            )
            * scale
        ).astype(jnp.bfloat16),
        "dp",
        scatter_dimension=0,
        tiled=True,
    ).astype(jnp.float32)
    return (act_out, grad_out, summed[None, None])


def solution(mesh):
    in_specs = (
        P("section", ("dp", "expert"), None),
        P("section", ("dp", "expert"), None),
        P("section", ("dp", "expert"), None),
        P("section", ("dp", "expert"), None),
        P("section", ("dp", "expert"), None),
        P("section", ("dp", "expert"), None),
        P("section", ("dp", "expert"), None),
        P("section", None),
        P("section", "expert", None, None),
        P("section", "expert", None, None),
        P("section", "expert", None, None),
    )
    out_specs = (
        P("section", ("dp", "expert"), None),
        P("section", ("dp", "expert"), None),
        P("section", "expert", "dp", None),
    )
    return jax.shard_map(shards, mesh=mesh, in_specs=in_specs, out_specs=out_specs, check_vma=False)
```

profile of v0, /device:TPU:0, one launch (start us, length us, event | category | flops | bytes accessed | tf_op | source)
XLA Modules:
  0.0 153.3 jit_solution(3169430178032927821)
XLA Ops:
  13.1 1.9 %mul.223 = f32[128,2048]{1,0:T(8,128)S(1)} reshape(f32[64,2,2048]{2,1,0:T(2,128)} %mul.222) | data formatting | bytes 2097152 | tf_op jit(solution)/shard_map/mul | solution.py:72
  16.9 14.5 %all_to_all.25 = bf16[4,40,2048]{2,1,0:T(8,128)(2,1)} all-to-all(bf16[4,40,2048]{2,1,0:T(8,128)(2,1)S(1)} %bitcast.103), channel_id=1, replica_groups=mesh['dp'=4,'section'=2,'expert'=4] {'expert'}, dimensions={0} | all-to-all | bytes 1310720 | tf_op jit(solution)/shard_map/all_to_all | solution.py:97
  31.4 4.2 %all-to-all-start.2 = ((bf16[4,40,2048]{2,1,0:T(8,128)(2,1)}), bf16[4,40,2048]{2,1,0:T(8,128)(2,1)}, u32[]{:S(2)}, u32[]{:S(2)}) async-start(bf16[4,40,2048]{2,1,0:T(8,128)(2,1)} %bitcast.102), calls=%async_computation.2 | async-start | bytes 1310720 | tf_op jit(solution)/shard_map/all_to_all | solution.py:98
  37.2 8.7 %all-to-all-done.2 = bf16[4,40,2048]{2,1,0:T(8,128)(2,1)} async-done(((bf16[4,40,2048]{2,1,0:T(8,128)(2,1)}), bf16[4,40,2048]{2,1,0:T(8,128)(2,1)}, u32[]{:S(2)}, u32[]{:S(2)}) %all-to-all-start.2) | async-done | bytes 655392 | tf_op jit(solution)/shard_map/all_to_all | solution.py:98
  45.9 2.3 %fusion.2 = f32[160,384]{1,0:T(8,128)S(1)} fusion(bf16[160,2048]{1,0:T(8,128)(2,1)} %bitcast.16, bf16[1,1,384,2048]{3,2,1,0:T(8,128)(2,1)} %param.21), kind=kOutput, calls=%fused_computation.9 | convolution fusion | flops 251658240 | bytes 2473984 | tf_op jit(solution)/shard_map/dot_general | solution.py:115
  49.5 5.6 %fusion = bf16[2048,1152]{1,0:T(8,128)(2,1)} fusion(bf16[160,2048]{1,0:T(8,128)(2,1)} %bitcast.16, bf16[160,2048]{1,0:T(8,128)(2,1)S(1)} %bitcast.107, bf16[160,384]{1,0:T(8,128)(2,1)S(1)} %get-tuple-element.5, bf16[160,384]{1,0:T(8,128)(2,1)S(1)} %broadcast_in_dim.16, bf16[160,384]{1,0:T(8,128)(2,1)S(1)} %get-tuple-element.7, ...), kind=kOutput, calls=%fused_computation.3 | convolution fusion | flops 1520975872 | bytes 6520832 | tf_op jit(solution)/shard_map/dot_general | solution.py:166
  61.2 3.7 %all-to-all-start.4 = ((bf16[4,40,2048]{2,1,0:T(8,128)(2,1)}), bf16[4,40,2048]{2,1,0:T(8,128)(2,1)S(1)}, u32[]{:S(2)}, u32[]{:S(2)}) async-start(bf16[4,40,2048]{2,1,0:T(8,128)(2,1)} %bitcast.19), calls=%async_computation.4 | async-start | bytes 1310720 | tf_op jit(solution)/shard_map/all_to_all | solution.py:132
  64.9 10.0 %all-to-all-done.4 = bf16[4,40,2048]{2,1,0:T(8,128)(2,1)S(1)} async-done(((bf16[4,40,2048]{2,1,0:T(8,128)(2,1)}), bf16[4,40,2048]{2,1,0:T(8,128)(2,1)S(1)}, u32[]{:S(2)}, u32[]{:S(2)}) %all-to-all-start.4) | async-done | bytes 655392 | tf_op jit(solution)/shard_map/all_to_all | solution.py:132
  74.9 1.7 %gather_fusion.1 = bf16[128,2048]{1,0:T(8,128)(2,1)} fusion(bf16[160,2048]{1,0:T(8,128)(2,1)S(1)} %bitcast.101, s32[1024]{0:T(1024)S(1)} %pad_clamp_fusion), kind=kCustom, calls=%fused_computation.1 | custom fusion | bytes 1049088 | tf_op jit(solution)/shard_map/gather | solution.py:145
  76.6 1.7 %reshape.237 = f32[64,2,2048]{2,1,0:T(2,128)S(1)} reshape(bf16[128,2048]{1,0:T(8,128)(2,1)} %gather_fusion.1) | data formatting | bytes 1572864 | tf_op jit(solution)/shard_map/convert_element_type | solution.py:145
  82.2 2.2 %reshape.221 = bf16[128,2048]{1,0:T(8,128)(2,1)} reshape(bf16[64,2,2048]{2,1,0:T(2,128)(2,1)} %broadcast_in_dim.13) | data formatting | bytes 1048576 | tf_op jit(solution)/shard_map/reshape | solution.py:80
  84.4 2.2 %convolution_convert_fusion.2 = bf16[160,2048]{1,0:T(8,128)(2,1)} fusion(bf16[128,2048]{1,0:T(8,128)(2,1)} %reshape.221, s32[128]{0:T(128)S(1)} %multiply_add_fusion.2), kind=kOutput, calls=%fused_computation.8 | convolution fusion | flops 84234240 | bytes 1180160 | tf_op jit(solution)/shard_map/dot_general | solution.py:78
  86.6 4.2 %all-to-all-start = ((bf16[4,40,2048]{2,1,0:T(8,128)(2,1)}), bf16[4,40,2048]{2,1,0:T(8,128)(2,1)}, u32[]{:S(2)}, u32[]{:S(2)}) async-start(bf16[4,40,2048]{2,1,0:T(8,128)(2,1)} %bitcast.104), calls=%async_computation | async-start | bytes 1310720 | tf_op jit(solution)/shard_map/all_to_all | solution.py:90
  91.1 9.9 %all-to-all-done = bf16[4,40,2048]{2,1,0:T(8,128)(2,1)} async-done(((bf16[4,40,2048]{2,1,0:T(8,128)(2,1)}), bf16[4,40,2048]{2,1,0:T(8,128)(2,1)}, u32[]{:S(2)}, u32[]{:S(2)}) %all-to-all-start) | async-done | bytes 655392 | tf_op jit(solution)/shard_map/all_to_all | solution.py:90
  101.1 2.3 %fusion.14 = f32[160,384]{1,0:T(8,128)} fusion(bf16[160,2048]{1,0:T(8,128)(2,1)} %bitcast.4, bf16[1,1,2048,384]{3,2,1,0:T(8,128)(2,1)S(1)} %copy-done.2), kind=kOutput, calls=%fused_computation.21 | convolution fusion | flops 251658240 | bytes 2473984 | tf_op jit(solution)/shard_map/dot_general | solution.py:103
  103.3 3.6 %convolution_convert_fusion.1 = bf16[160,2048]{1,0:T(8,128)(2,1)} fusion(bf16[1,1,384,2048]{3,2,1,0:T(8,128)(2,1)} %param.21, bf16[160,2048]{1,0:T(8,128)(2,1)} %bitcast.4, bf16[1,1,2048,384]{3,2,1,0:T(8,128)(2,1)S(1)} %copy-done, f32[160,384]{1,0:T(8,128)} %fusion.14), kind=kOutput, calls=%fused_computation.7 | convolution fusion | flops 504012800 | bytes 4702208 | tf_op jit(solution)/shard_map/dot_general | solution.py:106
  106.9 3.6 %all-to-all-start.1 = ((bf16[4,40,2048]{2,1,0:T(8,128)(2,1)}), bf16[4,40,2048]{2,1,0:T(8,128)(2,1)S(1)}, u32[]{:S(2)}, u32[]{:S(2)}) async-start(bf16[4,40,2048]{2,1,0:T(8,128)(2,1)} %bitcast.108), calls=%async_computation.1 | async-start | bytes 1310720 | tf_op jit(solution)/shard_map/all_to_all | solution.py:125
  111.5 1.9 %collective-permute-start.1 = (bf16[1,64,2048]{2,1,0:T(8,128)(2,1)}, bf16[1,64,2048]{2,1,0:T(8,128)(2,1)}, u32[]{:S(2)}, u32[]{:S(2)}) collective-permute-start(bf16[1,64,2048]{2,1,0:T(8,128)(2,1)} %fusion.49), channel_id=1, source_target_pairs={{4,0},{0,4},{5,1},{1,5},{6,2},{2,6},{7,3},{3,7},{12,8},{8,12},{13,... | collective-permute-start | bytes 786440 | tf_op jit(solution)/shard_map/ppermute | solution.py:18
  113.4 7.4 %all-to-all-done.1 = bf16[4,40,2048]{2,1,0:T(8,128)(2,1)S(1)} async-done(((bf16[4,40,2048]{2,1,0:T(8,128)(2,1)}), bf16[4,40,2048]{2,1,0:T(8,128)(2,1)S(1)}, u32[]{:S(2)}, u32[]{:S(2)}) %all-to-all-start.1) | async-done | bytes 655392 | tf_op jit(solution)/shard_map/all_to_all | solution.py:125
  124.0 1.9 %collective-permute-start = (bf16[1,64,2048]{2,1,0:T(8,128)(2,1)S(1)}, bf16[1,64,2048]{2,1,0:T(8,128)(2,1)S(1)}, u32[]{:S(2)}, u32[]{:S(2)}) collective-permute-start(bf16[1,64,2048]{2,1,0:T(8,128)(2,1)S(1)} %fusion.48), channel_id=1, source_target_pairs={{0,4},{4,0},{1,5},{5,1},{2,6},{6,2},{3,7},{7,3},{8,12},{12,8},{9,1... | collective-permute-start | bytes 786440 | tf_op jit(solution)/shard_map/ppermute | solution.py:15
  126.0 6.2 %collective-permute-done = bf16[1,64,2048]{2,1,0:T(8,128)(2,1)S(1)} collective-permute-done((bf16[1,64,2048]{2,1,0:T(8,128)(2,1)S(1)}, bf16[1,64,2048]{2,1,0:T(8,128)(2,1)S(1)}, u32[]{:S(2)}, u32[]{:S(2)}) %collective-permute-start) | collective-permute-done | bytes 262176 | tf_op jit(solution)/shard_map/ppermute | solution.py:15
  132.2 9.1 %reduce-scatter.2.cloned.1.call-done = bf16[512,1152]{1,0:T(8,128)(2,1)} async-done(((bf16[2048,1152]{1,0:T(8,128)(2,1)}), bf16[512,1152]{1,0:T(8,128)(2,1)}) %reduce-scatter.2.cloned.1.call-update) | async-done | bytes 1179664 | tf_op jit(solution)/shard_map/reduce_scatter | solution.py:164
  141.3 2.8 %bitcast_convert_fusion = f32[1,1,512,1152]{3,2,1,0:T(8,128)} fusion(bf16[512,1152]{1,0:T(8,128)(2,1)} %reduce-scatter.2.cloned.1.call-done), kind=kLoop, calls=%fused_computation.28 | loop fusion | flops 589824 | bytes 3538944 | tf_op jit(solution)/shard_map/broadcast_in_dim | solution.py:175
  144.8 1.7 %copy.29 = bf16[1,64,2048]{2,1,0:T(8,128)(2,1)} copy(bf16[1,64,2048]{2,1,0:T(8,128)(2,1)} %collective-permute-done.1) | data formatting | bytes 524288
  (95 shorter events, 25.5 us)
Async XLA Ops:
  7.2 41.1 %copy-start = (bf16[1,1,2048,384]{3,2,1,0:T(8,128)(2,1)S(1)}, bf16[1,1,2048,384]{3,2,1,0:T(8,128)(2,1)}, u32[]{:S(2)}) copy-start(bf16[1,1,2048,384]{3,2,1,0:T(8,128)(2,1)} %param.20) | copy-start | bytes 4718596
  7.2 4.3 %copy-start.9 = (bf16[1,64,2048]{2,1,0:T(8,128)(2,1)S(1)}, bf16[1,64,2048]{2,1,0:T(8,128)(2,1)}, u32[]{:S(2)}) copy-start(bf16[1,64,2048]{2,1,0:T(8,128)(2,1)} %param.13) | copy-start | bytes 786436
  8.7 1.1 copy-start.19
  11.5 3.5 %copy-start.17 = (f32[1,64,2]{1,2,0:T(2,128)S(1)}, f32[1,64,2]{1,2,0:T(2,128)}, u32[]{:S(2)}) copy-start(f32[1,64,2]{1,2,0:T(2,128)} %param.17) | copy-start | bytes 1540
  16.9 18.7 %copy-start.1 = (bf16[1,1,2048,384]{3,2,1,0:T(8,128)(2,1)S(1)}, bf16[1,1,2048,384]{3,2,1,0:T(8,128)(2,1)}, u32[]{:S(2)}) copy-start(bf16[1,1,2048,384]{3,2,1,0:T(8,128)(2,1)} %param.19) | copy-start | bytes 4718596
  31.4 14.5 %all-to-all-start.2 = ((bf16[4,40,2048]{2,1,0:T(8,128)(2,1)}), bf16[4,40,2048]{2,1,0:T(8,128)(2,1)}, u32[]{:S(2)}, u32[]{:S(2)}) async-start(bf16[4,40,2048]{2,1,0:T(8,128)(2,1)} %bitcast.102), calls=%async_computation.2 | async-start | bytes 1310720 | tf_op jit(solution)/shard_map/all_to_all | solution.py:98
  35.6 105.7 %reduce-scatter.2.cloned.1.call-start = ((), (), s32[]{:S(2)}) async-start(), calls=%async_computation.6 | async-start | bytes 5898240 | tf_op jit(solution)/shard_map/reduce_scatter | solution.py:164
  45.9 2.3 %copy-start.6 = (bf16[4,40,2048]{2,1,0:T(8,128)(2,1)S(1)}, bf16[4,40,2048]{2,1,0:T(8,128)(2,1)}, u32[]{:S(2)}) copy-start(bf16[4,40,2048]{2,1,0:T(8,128)(2,1)} %all_to_all.25) | copy-start | bytes 1966084
  55.1 1.4 copy-start.16
  55.1 2.1 %copy-start.7 = (bf16[1,64,2048]{2,1,0:T(8,128)(2,1)S(1)}, bf16[1,64,2048]{2,1,0:T(8,128)(2,1)}, u32[]{:S(2)}) copy-start(bf16[1,64,2048]{2,1,0:T(8,128)(2,1)} %param.11) | copy-start | bytes 786436
  57.2 2.4 %copy-start.12 = (bf16[160,384]{1,0:T(8,128)(2,1)S(1)}, bf16[160,384]{1,0:T(8,128)(2,1)}, u32[]{:S(2)}) copy-start(bf16[160,384]{1,0:T(8,128)(2,1)} %copy-done.11) | copy-start | bytes 368644
  61.2 13.7 %all-to-all-start.4 = ((bf16[4,40,2048]{2,1,0:T(8,128)(2,1)}), bf16[4,40,2048]{2,1,0:T(8,128)(2,1)S(1)}, u32[]{:S(2)}, u32[]{:S(2)}) async-start(bf16[4,40,2048]{2,1,0:T(8,128)(2,1)} %bitcast.19), calls=%async_computation.4 | async-start | bytes 1310720 | tf_op jit(solution)/shard_map/all_to_all | solution.py:132
  76.6 3.0 %copy-start.5 = (bf16[1,64,2048]{2,1,0:T(8,128)(2,1)S(1)}, bf16[1,64,2048]{2,1,0:T(8,128)(2,1)}, u32[]{:S(2)}) copy-start(bf16[1,64,2048]{2,1,0:T(8,128)(2,1)} %param.12) | copy-start | bytes 786436
  76.6 3.0 %copy-start.14 = (f32[1,2048]{1,0:T(1,128)S(1)}, f32[1,2048]{1,0:T(1,128)}, u32[]{:S(2)}) copy-start(f32[1,2048]{1,0:T(1,128)} %param.18) | copy-start | bytes 24580
  79.7 1.4 copy-start.3
  82.2 8.8 %copy-start.18 = (f32[1,64,2]{1,2,0:T(2,128)S(1)}, f32[1,64,2]{1,2,0:T(2,128)}, u32[]{:S(2)}) copy-start(f32[1,64,2]{1,2,0:T(2,128)} %param.16) | copy-start | bytes 1540
  82.2 18.9 %copy-start.2 = (bf16[1,1,2048,384]{3,2,1,0:T(8,128)(2,1)S(1)}, bf16[1,1,2048,384]{3,2,1,0:T(8,128)(2,1)}, u32[]{:S(2)}) copy-start(bf16[1,1,2048,384]{3,2,1,0:T(8,128)(2,1)} %param.19) | copy-start | bytes 4718596
  86.6 14.5 %all-to-all-start = ((bf16[4,40,2048]{2,1,0:T(8,128)(2,1)}), bf16[4,40,2048]{2,1,0:T(8,128)(2,1)}, u32[]{:S(2)}, u32[]{:S(2)}) async-start(bf16[4,40,2048]{2,1,0:T(8,128)(2,1)} %bitcast.104), calls=%async_computation | async-start | bytes 1310720 | tf_op jit(solution)/shard_map/all_to_all | solution.py:90
  103.3 7.2 %copy-start.10 = (bf16[1,64,2048]{2,1,0:T(8,128)(2,1)S(1)}, bf16[1,64,2048]{2,1,0:T(8,128)(2,1)}, u32[]{:S(2)}) copy-start(bf16[1,64,2048]{2,1,0:T(8,128)(2,1)} %param.13) | copy-start | bytes 786436
  106.9 3.7 %copy-start.4 = (f32[64,2048]{1,0:T(8,128)S(1)}, f32[64,2048]{1,0:T(8,128)}, u32[]{:S(2)}) copy-start(f32[64,2048]{1,0:T(8,128)} %copy-done.3) | copy-start | bytes 1572868
  106.9 13.8 %all-to-all-start.1 = ((bf16[4,40,2048]{2,1,0:T(8,128)(2,1)}), bf16[4,40,2048]{2,1,0:T(8,128)(2,1)S(1)}, u32[]{:S(2)}, u32[]{:S(2)}) async-start(bf16[4,40,2048]{2,1,0:T(8,128)(2,1)} %bitcast.108), calls=%async_computation.1 | async-start | bytes 1310720 | tf_op jit(solution)/shard_map/all_to_all | solution.py:125
  111.5 14.4 %collective-permute-start.1 = (bf16[1,64,2048]{2,1,0:T(8,128)(2,1)}, bf16[1,64,2048]{2,1,0:T(8,128)(2,1)}, u32[]{:S(2)}, u32[]{:S(2)}) collective-permute-start(bf16[1,64,2048]{2,1,0:T(8,128)(2,1)} %fusion.49), channel_id=1, source_target_pairs={{4,0},{0,4},{5,1},{1,5},{6,2},{2,6},{7,3},{3,7},{12,8},{8,12},{13,... | collective-permute-start | bytes 786440 | tf_op jit(solution)/shard_map/ppermute | solution.py:18
  121.7 2.2 %copy-start.8 = (bf16[1,64,2048]{2,1,0:T(8,128)(2,1)S(1)}, bf16[1,64,2048]{2,1,0:T(8,128)(2,1)}, u32[]{:S(2)}) copy-start(bf16[1,64,2048]{2,1,0:T(8,128)(2,1)} %param.11) | copy-start | bytes 786436
  124.0 8.2 %collective-permute-start = (bf16[1,64,2048]{2,1,0:T(8,128)(2,1)S(1)}, bf16[1,64,2048]{2,1,0:T(8,128)(2,1)S(1)}, u32[]{:S(2)}, u32[]{:S(2)}) collective-permute-start(bf16[1,64,2048]{2,1,0:T(8,128)(2,1)S(1)} %fusion.48), channel_id=1, source_target_pairs={{0,4},{4,0},{1,5},{5,1},{2,6},{6,2},{3,7},{7,3},{8,12},{12,8},{9,1... | collective-permute-start | bytes 786440 | tf_op jit(solution)/shard_map/ppermute | solution.py:15
  (3 other events, 2.0 us)
Sparse Core Ops, SparseCore 0:
  55.3 85.9 reduce-scatter.1
where the time goes:
time: 154 us; the launch traced here: 153 us
  waiting for transfers between devices  51.3 us (33%)
  matrix products  21.8 us (14%)
  local copies, waits for them, and re-layouts  19.7 us (13%)
  starting transfers between devices  19.5 us (13%)
  blocking collectives  14.5 us (9%)
  between operations  14.5 us (9%)
  other arithmetic  12.1 us (8%)
    all_to_all x1, blocking collectives, shards(): lax.all_to_all(send_bwd, 'expert', split_axis=0, concat_axis=0, tiled=True)  14.5 us
    all_to_all x1, waiting for transfers between devices, shards(): lax.all_to_all(slot_grad.reshape(experts, capacity, width), 'expert', spl...  10 us
    all_to_all x1, waiting for transfers between devices, shards(): lax.all_to_all(send_fwd.reshape(experts, capacity, width), 'expert', spli...  9.94 us
    reduce_scatter x1, waiting for transfers between devices, shards(): lax.psum_scatter((lax.dot_general(left_rows, right_blocks, contract_first...  9.1 us
    all_to_all x1, waiting for transfers between devices, shards(): lax.all_to_all(send_grad, 'expert', split_axis=0, concat_axis=0, tiled=True)  8.66 us
    all_to_all x1, waiting for transfers between devices, shards(): lax.all_to_all(out_fwd.reshape(experts, capacity, width), 'expert', split...  7.38 us
    ppermute x1, waiting for transfers between devices, padded(): lax.ppermute(lax.slice_in_dim(block, block.shape[dim] - width, None, axis...  6.21 us
    dot_general x1, matrix products, shards(): lax.dot_general(left_rows, right_blocks, contract_first, preferred_elemen...  5.61 us
  transfers between devices with their start and end apart: 7, of which 6 were waited for; matrix products, arithmetic and copies ran while one was open for 19% of the time, Pallas kernels for 0%

commit v1 on v0

v1 whole, which is shorter than its diff:
```python
import functools

import jax
import jax.numpy as jnp
from jax import lax
from jax.experimental import pallas as pl
from jax.experimental.pallas import tpu as pltpu
from jax.sharding import PartitionSpec as P

EPS = 1e-06
MESH = pl.DeviceIdType.MESH
F32 = jnp.float32
BF16 = jnp.bfloat16
LAST = (((1,), (1,)), ((), ()))
FIRST = (((0,), (0,)), ((), ()))


def bits_of(n):
    return [1 << b for b in reversed(range(n.bit_length() - 1))]


def lowest(m):
    return m & -m


def arrival_order(n):
    return sorted(range(1, n), key=lambda m: (-lowest(m), m))


class Copies:
    def __init__(self, send, recv):
        self.send, self.recv, self.names = send, recv, {}

    def make(self, name, src, dst, peer):
        i = self.names.setdefault(name, len(self.names))
        return pltpu.make_async_remote_copy(
            src_ref=src,
            dst_ref=dst,
            send_sem=self.send.at[i],
            recv_sem=self.recv.at[i],
            device_id=peer,
            device_id_type=MESH,
        )


def kernel(
    dims,
    act_ref, saved_ref, grad_ref, fids_ref, bids_ref, fgate_ref, bgate_ref, gain_ref,
    wg_hbm, wu_hbm, wd_hbm,
    act_out, grad_out, wgrad,
    wg, wu, wd, xb, xf, gates, rank, left, right, slot, outf, rs_slot, rs_outf, lay, inp,
    send_sems, recv_sems, w_sems,
):
    n_e, n_z, n_s, cap = dims
    tok, width = act_ref.shape
    hid = wg.shape[1]
    topk = fids_ref.shape[1]
    e = lax.axis_index("expert")
    z = lax.axis_index("dp")
    s = lax.axis_index("section")
    t_all = n_e * tok
    slots = n_e * cap
    blk = width // n_z
    cp = Copies(send_sems, recv_sems)
    sent = []

    loads = [
        pltpu.make_async_copy(a, b, w_sems.at[i])
        for i, (a, b) in enumerate(((wg_hbm, wg), (wu_hbm, wu), (wd_hbm, wd)))
    ]
    barrier = pltpu.get_barrier_semaphore()
    peers = [{"expert": e ^ b} for b in bits_of(n_e)]
    peers += [{"dp": lax.rem(z + o, n_z)} for o in range(1, n_z)]
    nxt = {"section": lax.rem(s + 1, n_s)}
    prv = {"section": lax.rem(s + n_s - 1, n_s)}
    peers += [nxt] if n_s == 2 else [nxt, prv]
    for peer in peers:
        pl.semaphore_signal(barrier, inc=1, device_id=peer, device_id_type=MESH)
    for c in loads:
        c.start()

    def rows(b):
        return pl.ds(pl.multiple_of(b * tok, tok), tok)

    def zrows(src):
        return pl.ds(pl.multiple_of(src * t_all, t_all), t_all)

    def lrows(src_z, src_e):
        return pl.ds(pl.multiple_of((src_z * n_e + src_e) * tok, tok), tok)

    def cols(d):
        return pl.ds(pl.multiple_of(d * blk, blk), blk)

    gain = gain_ref[...]

    def factor(x):
        return lax.rsqrt(jnp.mean(x * x, axis=1, keepdims=True) + EPS)

    saved = saved_ref[...].astype(F32)
    xb[0, rows(e), :] = (saved * factor(saved) * gain).astype(BF16)
    xb[1, rows(e), :] = grad_ref[...]
    act = act_ref[...].astype(F32)
    xf[rows(e), :] = (act * factor(act) * gain).astype(BF16)
    lane = lax.broadcasted_iota(jnp.int32, (tok, 128), 1)
    g = jnp.zeros((tok, 128), F32)
    hit = jnp.zeros((tok, 128), F32)
    for k in range(topk):
        g += jnp.where(lane == fids_ref[:, k : k + 1], fgate_ref[:, k : k + 1], 0.0)
        g += jnp.where(lane == bids_ref[:, k : k + 1] + 64, bgate_ref[:, k : k + 1], 0.0)
        hit += jnp.where(lane == bids_ref[:, k : k + 1], 1.0, 0.0)
    gates[rows(e), :] = g
    tri = (
        lax.broadcasted_iota(jnp.int32, (tok, tok), 0)
        >= lax.broadcasted_iota(jnp.int32, (tok, tok), 1)
    ).astype(F32).astype(BF16)
    upto = jnp.dot(tri, hit.astype(BF16), preferred_element_type=F32)
    rank[lrows(z, e), :] = (hit * upto).astype(BF16)

    pl.semaphore_wait(barrier, len(peers))

    def spread(name, ref, m):
        below = [b for b in bits_of(n_e) if m == 0 or b < lowest(m)]
        for b in below:
            c = cp.make((name, m, b), ref(e ^ m), ref(e ^ m), {"expert": e ^ b})
            c.start()
            sent.append(c)

    def arrived(name, ref, m):
        b = lowest(m)
        cp.make((name, m ^ b, b), ref(e ^ m), ref(e ^ m), {"expert": e ^ b}).wait_recv()

    def ref_b(b):
        return xb.at[:, rows(b), :]

    def ref_f(b):
        return xf.at[rows(b), :]

    def ref_g(b):
        return gates.at[rows(b), :]

    order = arrival_order(n_e)
    spread("g", ref_g, 0)
    spread("b", ref_b, 0)
    for o in range(1, n_z):
        d = lax.rem(z + o, n_z)
        for name, src, dst in (
            ("l", xb.at[:, rows(e), cols(d)], left.at[:, lrows(z, e), :]),
            ("r", rank.at[lrows(z, e), :], rank.at[lrows(z, e), :]),
        ):
            c = cp.make((name, "z", o), src, dst, {"dp": d})
            c.start()
            sent.append(c)

    for i, m in enumerate(order):
        arrived("g", ref_g, m)
        spread("g", ref_g, m)
        arrived("b", ref_b, m)
        spread("b", ref_b, m)
        if i == 0:
            spread("f", ref_f, 0)

    def ref_r0(b):
        return rank.at[lrows(z, b), :]

    spread("r0", ref_r0, 0)
    for m in order:
        arrived("r0", ref_r0, m)
        spread("r0", ref_r0, m)
    for c in loads:
        c.wait()

    lanes = lax.broadcasted_iota(jnp.int32, (t_all, 128), 1)

    def column(v, which):
        return jnp.sum(jnp.where(lanes == which, v, 0.0), axis=1, keepdims=True)

    def one_hot(src):
        r = column(rank[zrows(src), :].astype(F32), e)
        at = lax.broadcasted_iota(jnp.int32, (t_all, slots), 1)
        block = lax.broadcasted_iota(jnp.int32, (t_all, slots), 0) // tok
        want = r.astype(jnp.int32) - 1 + block * cap
        return jnp.where((at == want) & (r > 0.5), 1.0, 0.0).astype(BF16)

    gb = column(gates[...], e + 64)
    nb = xb[0]
    pg = jnp.dot(nb, wg[...], preferred_element_type=F32)
    pu = jnp.dot(nb, wu[...], preferred_element_type=F32)
    hg = gb * lax.dot_general(xb[1], wd[...], LAST, preferred_element_type=F32)
    sig = 1.0 / (1.0 + jnp.exp(-pg))
    silu = pg * sig
    gg = (hg * pu * sig * (1.0 + pg * (1.0 - sig))).astype(BF16)
    ug = (hg * silu).astype(BF16)
    hb = (gb * silu * pu).astype(BF16)
    own = one_hot(z)
    for i, v in enumerate((gg, ug, hb)):
        right[z, i] = lax.dot_general(own, v, FIRST, preferred_element_type=F32).astype(BF16)

    def pass_on(way, hop, i, start):
        src = z - hop * way
        if start:
            ok = (z + way >= 0) & (z + way < n_z) & (src >= 0) & (src < n_z)
            peer = z + way
        else:
            ok = (src - way >= 0) & (src - way < n_z) & (z + way >= 0)
            peer = z + way
        src = jnp.clip(src, 0, n_z - 1)
        peer = jnp.clip(peer, 0, n_z - 1)
        return ok, cp.make(
            ("x", way, hop, i), right.at[src, i], right.at[src, i], {"dp": peer}
        )

    relayed = []

    def relay_start(hop):
        for i in range(3):
            for way in (1, -1):
                ok, c = pass_on(way, hop, i, True)
                pl.when(ok)(c.start)
                relayed.append((ok, c))

    def relay_wait(hop):
        for i in range(3):
            for way in (1, -1):
                src = z - hop * way
                ok = (src >= 0) & (src < n_z)
                at = jnp.clip(src, 0, n_z - 1)
                c = cp.make(
                    ("x", way, hop - 1, i), right.at[at, i], right.at[at, i],
                    {"dp": jnp.clip(z + way, 0, n_z - 1)},
                )
                pl.when(ok)(c.wait_recv)

    relay_start(0)

    half = 512
    for j in range(width // half):
        at = slice(j * half, (j + 1) * half)
        v = lax.dot_general(gg, wg[at, :], LAST, preferred_element_type=F32)
        v += lax.dot_general(ug, wu[at, :], LAST, preferred_element_type=F32)
        slot[:, at] = v.astype(BF16)

    def blocks(b):
        return [m for m in range(0, n_e, 2 * b)]

    def place(b):
        return sum(len(blocks(c)) for c in bits_of(n_e) if c < b)

    def reduce_send(name, part, land, b):
        for i, m in enumerate(blocks(b)):
            c = cp.make(
                (name, b, m), part.at[rows(e ^ b ^ m), :], land.at[place(b) + i],
                {"expert": e ^ b},
            )
            c.start()
            sent.append(c)

    def reduce_wait(name, part, land, b):
        for i, m in enumerate(blocks(b)):
            to = land.at[place(b) + i]
            cp.make((name, b, m), part.at[rows(e ^ b ^ m), :], to, {"expert": e ^ b}).wait_recv()

    def reduce_add(part, land, b):
        for i, m in enumerate(blocks(b)):
            v = part[rows(e ^ m), :].astype(F32) + land[place(b) + i].astype(F32)
            part[rows(e ^ m), :] = v.astype(BF16)

    up = list(reversed(bits_of(n_e)))
    reduce_send("s", slot, rs_slot, up[0])

    for m in order:
        arrived("f", ref_f, m)
        spread("f", ref_f, m)
    gf = column(gates[...], e)
    nf = xf[...]
    fg = jnp.dot(nf, wg[...], preferred_element_type=F32)
    fu = jnp.dot(nf, wu[...], preferred_element_type=F32)
    hf = (gf * (fg / (1.0 + jnp.exp(-fg))) * fu).astype(BF16)
    for j in range(width // half):
        at = slice(j * half, (j + 1) * half)
        outf[:, at] = jnp.dot(hf, wd[:, at], preferred_element_type=F32).astype(BF16)
    reduce_send("o", outf, rs_outf, up[0])
    for b, nb_ in zip(up[:-1], up[1:]):
        for name, part, land in (("s", slot, rs_slot), ("o", outf, rs_outf)):
            reduce_wait(name, part, land, b)
            reduce_add(part, land, b)
            reduce_send(name, part, land, nb_)

    def ref_l(o):
        return lambda b: left.at[:, lrows(lax.rem(z + n_z - o, n_z), b), :]

    def ref_r(o):
        return lambda b: rank.at[lrows(lax.rem(z + n_z - o, n_z), b), :]

    for o in range(1, n_z):
        d = lax.rem(z + o, n_z)
        cp.make(
            ("l", "z", o), xb.at[:, rows(e), cols(d)], ref_l(o)(e), {"dp": d}
        ).wait_recv()
        cp.make(("r", "z", o), rank.at[lrows(z, e), :], ref_r(o)(e), {"dp": d}).wait_recv()
        spread(("l", o), ref_l(o), 0)
        spread(("r", o), ref_r(o), 0)

    left[:, zrows(z), :] = xb[:, :, cols(z)]
    scale = 1.0 / n_z

    def add(src, first=False):
        p = one_hot(src)
        for i in range(3):
            at = slice(i * hid, (i + 1) * hid)
            r = jnp.dot(p, right[src, i], preferred_element_type=F32).astype(BF16)
            v = lax.dot_general(
                left[i // 2, zrows(src), :], r, FIRST, preferred_element_type=F32
            ) * scale
            wgrad[:, at] = v if first else wgrad[:, at] + v

    add(z, True)
    relay_wait(1)
    if n_z > 2:
        relay_start(1)

    last = up[-1]
    reduce_wait("s", slot, rs_slot, last)
    ng = (slot[rows(e), :].astype(F32) + rs_slot[place(last)].astype(F32)) * gain
    x = saved_ref[...].astype(F32)
    f = factor(x)
    dot = jnp.mean(x * ng, axis=1, keepdims=True)
    inp[...] = (grad_ref[...].astype(F32) + f * ng - x * (f * f * f * dot)).astype(BF16)
    c_in = cp.make("grad", inp, grad_out, prv)
    c_in.start()
    reduce_wait("o", outf, rs_outf, last)
    lay[...] = (
        act_ref[...].astype(F32)
        + outf[rows(e), :].astype(F32)
        + rs_outf[place(last)].astype(F32)
    ).astype(BF16)
    c_act = cp.make("act", lay, act_out, nxt)
    c_act.start()

    for m in order:
        for o in range(1, n_z):
            for name, ref in (("l", ref_l), ("r", ref_r)):
                arrived((name, o), ref(o), m)
                spread((name, o), ref(o), m)

    for hop in range(1, n_z):
        if hop > 1:
            relay_wait(hop)
            if hop < n_z - 1:
                relay_start(hop)
        for way in (1, -1):
            src = z - hop * way

            @pl.when((src >= 0) & (src < n_z))
            def _():
                add(jnp.clip(src, 0, n_z - 1))

    c_in.wait()
    c_act.wait()
    for c in sent:
        c.wait_send()
    for ok, c in relayed:
        pl.when(ok)(c.wait_send)


def shards(*args):
    n_e, n_z, n_s = (lax.axis_size(a) for a in ("expert", "dp", "section"))
    (act, saved, grad, fids, bids, fgate, bgate) = (a[0] for a in args[:7])
    gain = args[7]
    wg, wu, wd = (a[0, 0] for a in args[8:])
    tok, width = act.shape
    hid = wg.shape[1]
    topk = fids.shape[1]
    cap = min(tok, 5 * tok * topk // (4 * n_e))
    t_all = n_e * tok
    blk = width // n_z
    steps = n_e.bit_length() - 1
    n_copies = 4 * (n_e - 1) + (n_z - 1) * 2 * n_e + 6 * (n_z - 1) + 2 * (n_e - 1) + 2 + steps
    vmem = pl.BlockSpec(memory_space=pltpu.VMEM)
    hbm = pl.BlockSpec(memory_space=pl.ANY)
    act_out, grad_out, wgrad = pl.pallas_call(
        functools.partial(kernel, (n_e, n_z, n_s, cap)),
        out_shape=(
            jax.ShapeDtypeStruct((tok, width), BF16),
            jax.ShapeDtypeStruct((tok, width), BF16),
            jax.ShapeDtypeStruct((blk, 3 * hid), F32),
        ),
        in_specs=[vmem] * 8 + [hbm] * 3,
        out_specs=[vmem] * 3,
        scratch_shapes=[
            pltpu.VMEM((width, hid), BF16),
            pltpu.VMEM((width, hid), BF16),
            pltpu.VMEM((hid, width), BF16),
            pltpu.VMEM((2, t_all, width), BF16),
            pltpu.VMEM((t_all, width), BF16),
            pltpu.VMEM((t_all, 128), F32),
            pltpu.VMEM((n_z * t_all, 128), BF16),
            pltpu.VMEM((2, n_z * t_all, blk), BF16),
            pltpu.VMEM((n_z, 3, n_e * cap, hid), BF16),
            pltpu.VMEM((t_all, width), BF16),
            pltpu.VMEM((t_all, width), BF16),
            pltpu.VMEM((n_e - 1, tok, width), BF16),
            pltpu.VMEM((n_e - 1, tok, width), BF16),
            pltpu.VMEM((tok, width), BF16),
            pltpu.VMEM((tok, width), BF16),
            pltpu.SemaphoreType.DMA((n_copies,)),
            pltpu.SemaphoreType.DMA((n_copies,)),
            pltpu.SemaphoreType.DMA((3,)),
        ],
        compiler_params=pltpu.CompilerParams(
            collective_id=0, has_side_effects=True, vmem_limit_bytes=60 * 1024 * 1024
        ),
    )(act, saved, grad, fids, bids, fgate, bgate, gain, wg, wu, wd)
    return act_out[None], grad_out[None], wgrad[None, None]


def solution(mesh):
    tokens = P("section", ("dp", "expert"), None)
    weights = P("section", "expert", None, None)
    in_specs = (tokens,) * 7 + (P("section", None),) + (weights,) * 3
    out_specs = (tokens, tokens, P("section", "expert", "dp", None))
    return jax.shard_map(shards, mesh=mesh, in_specs=in_specs, out_specs=out_specs, check_vma=False)
```

time: 154 us -> 86.4 us (0.56)
  Pallas kernels: 0 us -> 73.4 us
  waiting for transfers between devices: 51.3 us -> 0 us
  matrix products: 21.8 us -> 0 us
  starting transfers between devices: 19.5 us -> 0 us
  blocking collectives: 14.5 us -> 0 us
  between operations: 14.5 us -> 0.64 us
  other arithmetic: 12.1 us -> 0 us
  local copies, waits for them, and re-layouts: 19.7 us -> 12.1 us
    pallas_call x0 -> x1, Pallas kernels: none -> 73.4 us  [shards(): pl.pallas_call(functools.partial(kernel, (n_e, n_z, n_s, cap)), out_shape...]
    all_to_all x4 -> x0, waiting for transfers between devices: 36 us -> none  [the longest x1 10 us: shards(): lax.all_to_all(slot_grad.reshape(experts, capacity, width), 'expert', spl...]
    dot_general x10 -> x0, matrix products: 21.8 us -> none  [the longest x1 5.61 us: shards(): lax.dot_general(left_rows, right_blocks, contract_first, preferred_elemen...]
    all_to_all x4 -> x0, starting transfers between devices: 15.6 us -> none  [the longest x1 4.17 us: shards(): lax.all_to_all(send_grad, 'expert', split_axis=0, concat_axis=0, tiled=True)]
    all_to_all x1 -> x0, blocking collectives: 14.5 us -> none  [shards(): lax.all_to_all(send_bwd, 'expert', split_axis=0, concat_axis=0, tiled=True)]
    reduce_scatter x1 -> x0, waiting for transfers between devices: 9.1 us -> none  [shards(): lax.psum_scatter((lax.dot_general(left_rows, right_blocks, contract_first...]
    ppermute x2 -> x0, waiting for transfers between devices: 6.21 us -> none  [the longest x1 6.21 us: padded(): lax.ppermute(lax.slice_in_dim(block, block.shape[dim] - width, None, axis...]
    reduce_sum x7 -> x0, other arithmetic: 5.8 us -> none  [the longest x1 1.54 us: shards(): jnp.sum(fwd_gates[0][:, :, None] * picked, axis=1)]
  transfers between devices with their start and end apart: 7 -> 0, of which waited for: 6 -> 0; matrix products, arithmetic and copies ran while one was open for 19% -> 0% of each run, Pallas kernels for 0% -> 0%
where the time goes in v1:
time: 86.4 us; the launch traced here: 86.1 us
  Pallas kernels  73.4 us (85%)
  local copies, waits for them, and re-layouts  12.1 us (14%)
    pallas_call x1, Pallas kernels, shards(): pl.pallas_call(functools.partial(kernel, (n_e, n_z, n_s, cap)), out_shape...  73.4 us
    unnamed x3, local copies, waits for them, and re-layouts  6.56 us
    squeeze x4, local copies, waits for them, and re-layouts, shards(): act, saved, grad, fids, bids, fgate, bgate = (a[0] for a in args[:7])  5.52 us

profile of v1, /device:TPU:0, one launch (start us, length us, event | category | flops | bytes accessed | tf_op | source)
XLA Modules:
  0.0 86.1 jit_solution(309488057872812275)
XLA Ops:
  0.6 1.4 %copy.14.fids_ref = s32[64,2]{1,0:T(8,128)} copy(s32[64,2]{0,1:T(2,128)} %bitcast.22) | data formatting | bytes 1024 | tf_op jit(solution)/shard_map/squeeze | solution.py:367
  2.0 1.4 %copy.15.bids_ref = s32[64,2]{1,0:T(8,128)} copy(s32[64,2]{0,1:T(2,128)} %bitcast.23) | data formatting | bytes 1024 | tf_op jit(solution)/shard_map/squeeze | solution.py:367
  3.4 1.4 %copy.16.fgate_ref = f32[64,2]{1,0:T(8,128)} copy(f32[64,2]{0,1:T(2,128)} %bitcast.24) | data formatting | bytes 1024 | tf_op jit(solution)/shard_map/squeeze | solution.py:367
  4.8 1.4 %copy.17.bgate_ref = f32[64,2]{1,0:T(8,128)} copy(f32[64,2]{0,1:T(2,128)} %bitcast.25) | data formatting | bytes 1024 | tf_op jit(solution)/shard_map/squeeze | solution.py:367
  6.2 73.4 %shard_map.130 = (bf16[64,2048]{1,0:T(8,128)(2,1)}, bf16[64,2048]{1,0:T(8,128)(2,1)}, f32[512,1152]{1,0:T(8,128)}) custom-call(bf16[64,2048]{1,0:T(8,128)(2,1)} %bitcast.17, bf16[64,2048]{1,0:T(8,128)(2,1)} %bitcast.18, bf16[64,2048]{1,0:T(8,128)(2,1)} %bitcast.19, s32[64,2]{1,0:T(8,128)} %copy.14.fids_ref, s32[64,2]{1,0:T(8,128)} %copy.15.bids_ref, ...), custom_call_target="tpu_custom_call" | custom-call | tf_op jit(solution)/shard_map/pallas_call | solution.py:380
  79.6 1.7 %copy.21 = bf16[1,64,2048]{2,1,0:T(8,128)(2,1)} copy(bf16[1,64,2048]{2,1,0:T(8,128)(2,1)} %bitcast.21) | data formatting | bytes 524288
  81.3 1.7 %copy.22 = bf16[1,64,2048]{2,1,0:T(8,128)(2,1)} copy(bf16[1,64,2048]{2,1,0:T(8,128)(2,1)} %bitcast.20) | data formatting | bytes 524288
  82.9 3.2 %copy.23 = f32[1,1,512,1152]{3,2,1,0:T(8,128)} copy(f32[1,1,512,1152]{3,2,1,0:T(8,128)} %bitcast.13) | data formatting | bytes 4718592

commit v2 on v1

--- a/solution.py
+++ b/solution.py
@@ -54,7 +54,7 @@
     n_e, n_z, n_s, cap = dims
     tok, width = act_ref.shape
     hid = wg.shape[1]
-    topk = fids_ref.shape[1]
+    topk = fids_ref.shape[0]
     e = lax.axis_index("expert")
     z = lax.axis_index("dp")
     s = lax.axis_index("section")
@@ -104,15 +104,21 @@
     lane = lax.broadcasted_iota(jnp.int32, (tok, 128), 1)
     g = jnp.zeros((tok, 128), F32)
     hit = jnp.zeros((tok, 128), F32)
+    down = lax.broadcasted_iota(jnp.int32, (tok, tok), 0)
+    across = lax.broadcasted_iota(jnp.int32, (tok, tok), 1)
+
+    def turned(ref, k):
+        row = ref[k : k + 1, :].astype(F32)
+        return jnp.sum(jnp.where(down == across, row, 0.0), axis=1, keepdims=True)
+
     for k in range(topk):
-        g += jnp.where(lane == fids_ref[:, k : k + 1], fgate_ref[:, k : k + 1], 0.0)
-        g += jnp.where(lane == bids_ref[:, k : k + 1] + 64, bgate_ref[:, k : k + 1], 0.0)
-        hit += jnp.where(lane == bids_ref[:, k : k + 1], 1.0, 0.0)
+        f_id = turned(fids_ref, k).astype(jnp.int32)
+        b_id = turned(bids_ref, k).astype(jnp.int32)
+        g += jnp.where(lane == f_id, turned(fgate_ref, k), 0.0)
+        g += jnp.where(lane == b_id + 64, turned(bgate_ref, k), 0.0)
+        hit += jnp.where(lane == b_id, 1.0, 0.0)
     gates[rows(e), :] = g
-    tri = (
-        lax.broadcasted_iota(jnp.int32, (tok, tok), 0)
-        >= lax.broadcasted_iota(jnp.int32, (tok, tok), 1)
-    ).astype(F32).astype(BF16)
+    tri = (down >= across).astype(F32).astype(BF16)
     upto = jnp.dot(tri, hit.astype(BF16), preferred_element_type=F32)
     rank[lrows(z, e), :] = (hit * upto).astype(BF16)
 
@@ -129,8 +135,8 @@
         b = lowest(m)
         cp.make((name, m ^ b, b), ref(e ^ m), ref(e ^ m), {"expert": e ^ b}).wait_recv()
 
-    def ref_b(b):
-        return xb.at[:, rows(b), :]
+    def ref_b(i):
+        return lambda b: xb.at[i, rows(b), :]
 
     def ref_f(b):
         return xf.at[rows(b), :]
@@ -140,7 +146,8 @@
 
     order = arrival_order(n_e)
     spread("g", ref_g, 0)
-    spread("b", ref_b, 0)
+    spread(("b", 1), ref_b(1), 0)
+    spread(("b", 0), ref_b(0), 0)
     for o in range(1, n_z):
         d = lax.rem(z + o, n_z)
         for name, src, dst in (
@@ -154,8 +161,9 @@
     for i, m in enumerate(order):
         arrived("g", ref_g, m)
         spread("g", ref_g, m)
-        arrived("b", ref_b, m)
-        spread("b", ref_b, m)
+        for a in (1, 0):
+            arrived(("b", a), ref_b(a), m)
+            spread(("b", a), ref_b(a), m)
         if i == 0:
             spread("f", ref_f, 0)
 
@@ -166,6 +174,21 @@
     for m in order:
         arrived("r0", ref_r0, m)
         spread("r0", ref_r0, m)
+    def ref_l(o):
+        return lambda b: left.at[:, lrows(lax.rem(z + n_z - o, n_z), b), :]
+
+    def ref_r(o):
+        return lambda b: rank.at[lrows(lax.rem(z + n_z - o, n_z), b), :]
+
+    for o in range(1, n_z):
+        d = lax.rem(z + o, n_z)
+        cp.make(
+            ("l", "z", o), xb.at[:, rows(e), cols(d)], ref_l(o)(e), {"dp": d}
+        ).wait_recv()
+        cp.make(("r", "z", o), rank.at[lrows(z, e), :], ref_r(o)(e), {"dp": d}).wait_recv()
+        spread(("l", o), ref_l(o), 0)
+        spread(("r", o), ref_r(o), 0)
+
     for c in loads:
         c.wait()
 
@@ -195,14 +218,10 @@
     for i, v in enumerate((gg, ug, hb)):
         right[z, i] = lax.dot_general(own, v, FIRST, preferred_element_type=F32).astype(BF16)
 
-    def pass_on(way, hop, i, start):
+    def pass_on(way, hop, i):
         src = z - hop * way
-        if start:
-            ok = (z + way >= 0) & (z + way < n_z) & (src >= 0) & (src < n_z)
-            peer = z + way
-        else:
-            ok = (src - way >= 0) & (src - way < n_z) & (z + way >= 0)
-            peer = z + way
+        peer = z + way
+        ok = (peer >= 0) & (peer < n_z) & (src >= 0) & (src < n_z)
         src = jnp.clip(src, 0, n_z - 1)
         peer = jnp.clip(peer, 0, n_z - 1)
         return ok, cp.make(
@@ -211,26 +230,23 @@
 
     relayed = []
 
-    def relay_start(hop):
+    def relay(hop):
         for i in range(3):
             for way in (1, -1):
-                ok, c = pass_on(way, hop, i, True)
-                pl.when(ok)(c.start)
-                relayed.append((ok, c))
-
-    def relay_wait(hop):
-        for i in range(3):
-            for way in (1, -1):
-                src = z - hop * way
-                ok = (src >= 0) & (src < n_z)
-                at = jnp.clip(src, 0, n_z - 1)
-                c = cp.make(
-                    ("x", way, hop - 1, i), right.at[at, i], right.at[at, i],
-                    {"dp": jnp.clip(z + way, 0, n_z - 1)},
-                )
-                pl.when(ok)(c.wait_recv)
-
-    relay_start(0)
+                if hop > 0:
+                    src = z - hop * way
+                    at = jnp.clip(src, 0, n_z - 1)
+                    here = cp.make(
+                        ("x", way, hop - 1, i), right.at[at, i], right.at[at, i],
+                        {"dp": jnp.clip(z + way, 0, n_z - 1)},
+                    )
+                    pl.when((src >= 0) & (src < n_z))(here.wait_recv)
+                if hop < n_z - 1:
+                    ok, c = pass_on(way, hop, i)
+                    pl.when(ok)(c.start)
+                    relayed.append((ok, c))
+
+    relay(0)
 
     half = 512
     for j in range(width // half):
@@ -285,21 +301,6 @@
             reduce_add(part, land, b)
             reduce_send(name, part, land, nb_)
 
-    def ref_l(o):
-        return lambda b: left.at[:, lrows(lax.rem(z + n_z - o, n_z), b), :]
-
-    def ref_r(o):
-        return lambda b: rank.at[lrows(lax.rem(z + n_z - o, n_z), b), :]
-
-    for o in range(1, n_z):
-        d = lax.rem(z + o, n_z)
-        cp.make(
-            ("l", "z", o), xb.at[:, rows(e), cols(d)], ref_l(o)(e), {"dp": d}
-        ).wait_recv()
-        cp.make(("r", "z", o), rank.at[lrows(z, e), :], ref_r(o)(e), {"dp": d}).wait_recv()
-        spread(("l", o), ref_l(o), 0)
-        spread(("r", o), ref_r(o), 0)
-
     left[:, zrows(z), :] = xb[:, :, cols(z)]
     scale = 1.0 / n_z
 
@@ -313,10 +314,13 @@
             ) * scale
             wgrad[:, at] = v if first else wgrad[:, at] + v
 
+    relay(1)
     add(z, True)
-    relay_wait(1)
-    if n_z > 2:
-        relay_start(1)
+    for m in order:
+        for o in range(1, n_z):
+            for name, ref in (("l", ref_l), ("r", ref_r)):
+                arrived((name, o), ref(o), m)
+                spread((name, o), ref(o), m)
 
     last = up[-1]
     reduce_wait("s", slot, rs_slot, last)
@@ -336,17 +340,11 @@
     c_act = cp.make("act", lay, act_out, nxt)
     c_act.start()
 
-    for m in order:
-        for o in range(1, n_z):
-            for name, ref in (("l", ref_l), ("r", ref_r)):
-                arrived((name, o), ref(o), m)
-                spread((name, o), ref(o), m)
-
+    if n_z > 3:
+        relay(2)
     for hop in range(1, n_z):
-        if hop > 1:
-            relay_wait(hop)
-            if hop < n_z - 1:
-                relay_start(hop)
+        if hop > 2 or hop == n_z - 1 > 1:
+            relay(hop)
         for way in (1, -1):
             src = z - hop * way
 
@@ -360,6 +358,24 @@
         c.wait_send()
     for ok, c in relayed:
         pl.when(ok)(c.wait_send)
+
+
+def copy_kernel(*refs):
+    n = len(refs) // 2
+    for src, dst in zip(refs[:n], refs[n:]):
+        dst[...] = src[...]
+
+
+def hand_on(*arrays):
+    steps = 4
+    specs = [pl.BlockSpec((a.shape[0] // steps, a.shape[1]), lambda i: (i, 0)) for a in arrays]
+    return pl.pallas_call(
+        copy_kernel,
+        out_shape=tuple(jax.ShapeDtypeStruct(a.shape, a.dtype) for a in arrays),
+        grid=(steps,),
+        in_specs=specs,
+        out_specs=specs,
+    )(*arrays)
 
 
 def shards(*args):
@@ -370,11 +386,12 @@
     tok, width = act.shape
     hid = wg.shape[1]
     topk = fids.shape[1]
+    small = [a.T for a in (fids, bids, fgate, bgate)]
     cap = min(tok, 5 * tok * topk // (4 * n_e))
     t_all = n_e * tok
     blk = width // n_z
     steps = n_e.bit_length() - 1
-    n_copies = 4 * (n_e - 1) + (n_z - 1) * 2 * n_e + 6 * (n_z - 1) + 2 * (n_e - 1) + 2 + steps
+    n_copies = 5 * (n_e - 1) + (n_z - 1) * 2 * n_e + 6 * (n_z - 1) + 2 * (n_e - 1) + 2 + steps
     vmem = pl.BlockSpec(memory_space=pltpu.VMEM)
     hbm = pl.BlockSpec(memory_space=pl.ANY)
     act_out, grad_out, wgrad = pl.pallas_call(
@@ -409,7 +426,8 @@
         compiler_params=pltpu.CompilerParams(
             collective_id=0, has_side_effects=True, vmem_limit_bytes=60 * 1024 * 1024
         ),
-    )(act, saved, grad, fids, bids, fgate, bgate, gain, wg, wu, wd)
+    )(act, saved, grad, *small, gain, wg, wu, wd)
+    act_out, grad_out, wgrad = hand_on(act_out, grad_out, wgrad)
     return act_out[None], grad_out[None], wgrad[None, None]
 
 

time: 86.4 us -> 68.8 us (0.80)
  local copies, waits for them, and re-layouts: 12.1 us -> 0 us
  Pallas kernels: 73.4 us -> 67.9 us
    pallas_call x1, Pallas kernels: 73.4 us -> 63.8 us  [shards(): pl.pallas_call(functools.partial(kernel, (n_e, n_z, n_s, cap)), out_shape...]
    unnamed x3 -> x0, local copies, waits for them, and re-layouts: 6.56 us -> none
    squeeze x4 -> x0, local copies, waits for them, and re-layouts: 5.52 us -> none  [shards(): act, saved, grad, fids, bids, fgate, bgate = (a[0] for a in args[:7])]
    pallas_call x0 -> x1, Pallas kernels: none -> 4.12 us  [hand_on(): pl.pallas_call(copy_kernel, out_shape=tuple((jax.ShapeDtypeStruct(a.shape...]
where the time goes in v2:
time: 68.8 us; the launch traced here: 68.6 us
  Pallas kernels  67.9 us (99%)
    pallas_call x1, Pallas kernels, shards(): pl.pallas_call(functools.partial(kernel, (n_e, n_z, n_s, cap)), out_shape...  63.8 us
    pallas_call x1, Pallas kernels, hand_on(): pl.pallas_call(copy_kernel, out_shape=tuple((jax.ShapeDtypeStruct(a.shape...  4.12 us

profile of v2, /device:TPU:0, one launch (start us, length us, event | category | flops | bytes accessed | tf_op | source)
XLA Modules:
  0.0 68.6 jit_solution(5732442764592284186)
XLA Ops:
  0.6 63.8 %shard_map.130 = (bf16[64,2048]{1,0:T(8,128)(2,1)}, bf16[64,2048]{1,0:T(8,128)(2,1)}, f32[512,1152]{1,0:T(8,128)}) custom-call(bf16[64,2048]{1,0:T(8,128)(2,1)} %bitcast.24, bf16[64,2048]{1,0:T(8,128)(2,1)} %bitcast.25, bf16[64,2048]{1,0:T(8,128)(2,1)} %bitcast.26, s32[2,64]{1,0:T(2,128)} %bitcast.27, s32[2,64]{1,0:T(2,128)} %bitcast.28, f32[2,64]{1,0:T(2,128)} %bitcast.29, ...), custom_call_target="tpu_custom_call" | custom-call | tf_op jit(solution)/shard_map/pallas_call | solution.py:397
  64.5 4.1 %shard_map.131 = (bf16[64,2048]{1,0:T(8,128)(2,1)}, bf16[64,2048]{1,0:T(8,128)(2,1)}, f32[512,1152]{1,0:T(8,128)}) custom-call(bf16[64,2048]{1,0:T(8,128)(2,1)} %get-tuple-element.9.refs_0_, bf16[64,2048]{1,0:T(8,128)(2,1)} %get-tuple-element.10.refs_1_, f32[512,1152]{1,0:T(8,128)} %get-tuple-element.11.refs_2_), custom_call_target="tpu_custom_call" | custom-call | tf_op jit(solution)/shard_map/pallas_call | solution.py:372
